TPU v7x, 512 devices: a whole 4x8x8 slice. The times are simulated.
512 devices in a mesh: island: 8 (over x, y_hi), fsdp: 64 (over y_lo, z, core).
Axes of the slice: x: 4, y: 8 (y_hi: 2, y_lo: 4; y = y_hi * 4 + y_lo), z: 8, core: 2. Of those that a mesh axis runs over, the one named last changes fastest.
Arguments:
- act_t: bfloat16 [6144, 65536], P(None, ('island', 'fsdp')), may hold values from -6 to 6
- cotangent: bfloat16 [65536, 512], P(('island', 'fsdp')), may hold values from -0.06591797 to 0.06591797
- inner_params: float32 [8, 4, 6144, 512], P('island', None, 'fsdp'), may hold values from -6 to 6
- outer_params: float32 [6144, 512], P('fsdp'), may hold values from -6 to 6
- momentum: float32 [6144, 512], P('fsdp'), may hold values from -3 to 3
- frag_index: int32 [4], replicated, may hold values from 0 to 3, each once
Outputs:
- weight_grad: float32 [8, 6144, 512], P('island', 'fsdp')
- input_grad: bfloat16 [6144, 65536], P(None, ('island', 'fsdp'))
- new_params: float32 [6144, 512], P('fsdp')
- new_momentum: float32 [6144, 512], P('fsdp')
Inputs may be any that keep to these rules, and one draw needn't show every extreme that they name: `frag_index`: each slot number appears once.
All inputs are finite; a program needn't handle non-finite values.
Results may differ from a plain program's by a relative error of at most 0.005.
Values may be sent and summed in bfloat16 or wider, within the bound.
A program may use at most 64 MiB of HBM per device.

v0:
```python
import jax
import jax.numpy as jnp
from jax import lax
from jax.sharding import PartitionSpec as P


def local(act_t, cotangent, inner_params, outer_params, momentum, frag_index):
    frag_slot = frag_index[0]
    train_slot = frag_index[1]
    held = inner_params[0]
    fragment = lax.dynamic_index_in_dim(held, frag_slot, 0, keepdims=False)
    trained = lax.dynamic_index_in_dim(held, train_slot, 0, keepdims=False).astype(jnp.bfloat16)
    islands = lax.axis_size("island")
    weighted = (outer_params - fragment) / float(islands)
    delta = lax.psum(weighted, "island")
    new_momentum = 0.9 * momentum + delta
    new_params = outer_params - 0.7 * (delta + 0.9 * new_momentum)
    feature_rows = lax.all_to_all(act_t, "fsdp", split_axis=0, concat_axis=1, tiled=True)
    weight_grad = jnp.dot(
        feature_rows,
        lax.all_gather(cotangent, "fsdp", axis=0, tiled=True),
        preferred_element_type=jnp.float32,
    )
    input_grad = lax.dot_general(
        lax.all_gather(trained, "fsdp", axis=0, tiled=True),
        cotangent,
        (((1,), (1,)), ((), ())),
        preferred_element_type=jnp.float32,
    ).astype(jnp.bfloat16)
    return (weight_grad[None], input_grad, new_params, new_momentum)


def solution(mesh):
    in_specs = (
        P(None, ("island", "fsdp")),
        P(("island", "fsdp"), None),
        P("island", None, "fsdp", None),
        P("fsdp", None),
        P("fsdp", None),
        P(),
    )
    out_specs = (
        P("island", "fsdp", None),
        P(None, ("island", "fsdp")),
        P("fsdp", None),
        P("fsdp", None),
    )
    return jax.shard_map(local, mesh=mesh, in_specs=in_specs, out_specs=out_specs, check_vma=False)
```

profile of v0, /device:TPU:1, one launch (start us, length us, event | category | flops | bytes accessed | tf_op | source)
XLA Modules:
  0.0 304.1 jit_solution(5227923595893692424)
XLA Ops:
  8.0 0.0 all-reduce.2.cloned.1.call-start
  8.0 1.3 fusion.8
  11.3 1.7 fusion.7
  13.0 0.0 all-reduce.2.cloned.1.call-update
  13.1 0.0 all-gather.6.cloned.1.call-start
  15.0 1.6 dynamic-slice_convert_fusion
  16.6 0.0 all-gather.6.cloned.1.call-update
  16.7 0.0 all-gather.4.cloned.1.call-start
  16.7 0.5 all-gather.4.cloned.1.call-update
  17.2 0.0 copy-start
  17.3 0.0 copy-start.2
  17.3 0.0 copy-start.1
  17.3 15.6 %all-to-all-start = ((bf16[64,96,128]{2,1,0:T(8,128)(2,1)}), bf16[64,96,128]{2,1,0:T(8,128)(2,1)S(1)}, u32[]{:S(2)}, u32[]{:S(2)}) async-start(bf16[64,96,128]{2,1,0:T(8,128)(2,1)} %bitcast.24), calls=%async_computation | async-start | bytes 3145728 | tf_op jit(solution)/shard_map/all_to_all | solution.py:18
  32.8 100.5 %all-reduce.2.cloned.1.call-done = f32[96,512]{1,0:T(8,128)} async-done(((f32[96,512]{1,0:T(8,128)}), f32[96,512]{1,0:T(8,128)}) %all-reduce.2.cloned.1.call-update) | async-done | bytes 196624 | tf_op jit(solution)/shard_map/psum | solution.py:15
  133.3 0.0 copy-done
  133.3 0.0 copy-done.2
  133.3 1.7 multiply_subtract_fusion
  135.0 31.3 %all-gather.6.cloned.1.call-done = bf16[1,1,6144,512]{3,2,1,0:T(8,128)(2,1)} async-done(((bf16[1,1,96,512]{3,2,1,0:T(8,128)(2,1)}), bf16[1,1,6144,512]{3,2,1,0:T(8,128)(2,1)}) %all-gather.6.cloned.1.call-update) | async-done | bytes 6291472 | tf_op jit(solution)/shard_map/all_gather | solution.py:25
  166.4 0.0 copy-done.1
  166.4 5.7 %convolution_convert_fusion = bf16[6144,128]{1,0:T(8,128)(2,1)} fusion(bf16[128,512]{1,0:T(8,128)(2,1)S(1)} %copy-done.1, bf16[1,1,6144,512]{3,2,1,0:T(8,128)(2,1)} %all-gather.6.cloned.1.call-done), kind=kOutput, calls=%fused_computation | convolution fusion | flops 806092800 | bytes 7995392 | tf_op jit(solution)/shard_map/dot_general | solution.py:24
  172.1 0.0 all-to-all-done
  172.1 119.1 %all-gather.4.cloned.1.call-done = bf16[8192,512]{1,0:T(8,128)(2,1)} async-done(((bf16[128,512]{1,0:T(8,128)(2,1)}), bf16[8192,512]{1,0:T(8,128)(2,1)}) %all-gather.4.cloned.1.call-update) | async-done | bytes 8388624 | tf_op jit(solution)/shard_map/all_gather | solution.py:21
  291.2 5.5 %fusion.4 = f32[1,96,512]{2,1,0:T(8,128)} fusion(bf16[8192,512]{1,0:T(8,128)(2,1)} %all-gather.4.cloned.1.call-done, bf16[64,96,128]{2,1,0:T(8,128)(2,1)S(1)} %all-to-all-done), kind=kOutput, calls=%fused_computation.5 | convolution fusion | flops 805306368 | bytes 10158080 | tf_op jit(solution)/shard_map/dot_general | solution.py:19
Async XLA Ops:
  8.0 125.3 %all-reduce.2.cloned.1.call-start = ((), (), s32[]{:S(2)}) async-start(), calls=%async_computation.2 | async-start | bytes 393216 | tf_op jit(solution)/shard_map/psum | solution.py:15
  13.1 153.3 %all-gather.6.cloned.1.call-start = ((), (), s32[]{:S(2)}) async-start(), calls=%async_computation.3 | async-start | bytes 6389760 | tf_op jit(solution)/shard_map/all_gather | solution.py:25
  16.7 274.5 %all-gather.4.cloned.1.call-start = ((), (), s32[]{:S(2)}) async-start(), calls=%async_computation.1 | async-start | bytes 8519680 | tf_op jit(solution)/shard_map/all_gather | solution.py:21
  17.2 116.1 %copy-start = (f32[96,512]{1,0:T(8,128)S(1)}, f32[96,512]{1,0:T(8,128)}, u32[]{:S(2)}) copy-start(f32[96,512]{1,0:T(8,128)} %param.9) | copy-start | bytes 589828
  17.3 116.1 %copy-start.2 = (f32[96,512]{1,0:T(8,128)S(1)}, f32[96,512]{1,0:T(8,128)}, u32[]{:S(2)}) copy-start(f32[96,512]{1,0:T(8,128)} %param.10) | copy-start | bytes 589828
  17.3 149.1 %copy-start.1 = (bf16[128,512]{1,0:T(8,128)(2,1)S(1)}, bf16[128,512]{1,0:T(8,128)(2,1)}, u32[]{:S(2)}) copy-start(bf16[128,512]{1,0:T(8,128)(2,1)} %param.7) | copy-start | bytes 393220
  17.3 154.8 %all-to-all-start = ((bf16[64,96,128]{2,1,0:T(8,128)(2,1)}), bf16[64,96,128]{2,1,0:T(8,128)(2,1)S(1)}, u32[]{:S(2)}, u32[]{:S(2)}) async-start(bf16[64,96,128]{2,1,0:T(8,128)(2,1)} %bitcast.24), calls=%async_computation | async-start | bytes 3145728 | tf_op jit(solution)/shard_map/all_to_all | solution.py:18
Sparse Core Ops, SparseCore 0:
  13.2 120.0 all-reduce.1
Sparse Core Ops, SparseCore 1:
  16.7 149.6 all-gather.5
  168.4 122.7 all-gather.3
where the time goes:
time: 305 us; the launch traced here: 304 us
  waiting for transfers between devices  251 us (82%)
  between operations  19.4 us (6%)
  starting transfers between devices  15.7 us (5%)
  matrix products  11.2 us (4%)
  other arithmetic  3.45 us (1%)
    all_gather x1, waiting for transfers between devices, local(): lax.all_gather(cotangent, 'fsdp', axis=0, tiled=True)  119 us
    psum x1, waiting for transfers between devices, local(): delta = lax.psum(weighted, 'island')  100 us
    all_gather x1, waiting for transfers between devices, local(): lax.all_gather(trained, 'fsdp', axis=0, tiled=True)  31.3 us
    all_to_all x1, starting transfers between devices, local(): lax.all_to_all(act_t, 'fsdp', split_axis=0, concat_axis=1, tiled=True)  15.6 us
  transfers between devices with their start and end apart: 4, of which 3 were waited for; matrix products, arithmetic and copies ran while one was open for 3% of the time, Pallas kernels for 0%

commit v1 on v0

v1 whole, which is shorter than its diff:
```python
import jax
import jax.numpy as jnp
from jax import lax
from jax.experimental import pallas as pl
from jax.experimental.pallas import tpu as pltpu
from jax.sharding import PartitionSpec as P

MESH = pl.DeviceIdType.MESH
KV = 512
TOK = 128
ROWS = 96
NZ = 8
NX = 4
HALF = NZ // 2
DIRS = (1, -1)


def chain(d, h):
    return HALF if d == h else HALF - 1


MESSAGES = [(d, h, j) for d in range(2) for h in range(2) for j in range(HALF) if j < chain(d, h)]
SUMS = [(d, u, r) for d in range(2) for u in range(2) for r in range(HALF) if HALF - r <= chain(d, u)]


def kernel(
    frag, x_hbm, g_hbm, inner_hbm, outer_hbm, mom_hbm,
    wg_out, ig_out, par_out, newmom_out,
    inner_v, outer_v, mom_v, gbuf, gt, xbuf, wbuf, osend, rs_send, rs_recv, fin, fin_send, fin_recv,
    arw, ar_recv, ar_mid, ar_mid_recv, ar_tot,
    local_sem, w_sem, g_sem, ag_sem, x_sem, o_sem, rs_sem, fin_sem, ar_sem, own_sem,
):
    island = lax.axis_index("island")
    me = lax.axis_index("fsdp")
    core = lax.rem(me, 2)
    z = lax.rem(me // 2, NZ)
    y = me // (2 * NZ)
    u = y // 2
    p = lax.rem(y, 2)
    ix = island // 2
    iy = lax.rem(island, 2)

    def at(yy, zz, cc):
        return (island, (yy * NZ + zz) * 2 + cc)

    def zoff(o):
        return lax.rem(z + (o + NZ), NZ)

    y_pair = y + 1 - 2 * p
    quad = [None, at(y, z, 1 - core), at(y_pair, z, core), at(y_pair, z, 1 - core)]
    quad_pc = [(p, core), (p, 1 - core), (1 - p, core), (1 - p, 1 - core)]
    far = at(lax.rem(y + 2, 4), z, core)
    ring = [at(y, zoff(1), core), at(y, zoff(-1), core)]
    xs = [lax.rem(ix + k, NX) for k in range(NX)]
    xdev = [None] + [(xs[k] * 2 + iy, me) for k in range(1, NX)]
    ydev = (ix * 2 + 1 - iy, me)

    loads = [
        pltpu.make_async_copy(inner_hbm.at[0], inner_v, local_sem.at[0]),
        pltpu.make_async_copy(g_hbm, gbuf.at[0], local_sem.at[1]),
        pltpu.make_async_copy(x_hbm.at[:, p, :, core], xbuf.at[0], local_sem.at[2]),
        pltpu.make_async_copy(outer_hbm, outer_v, local_sem.at[3]),
        pltpu.make_async_copy(mom_hbm, mom_v, local_sem.at[4]),
    ]
    for c in loads:
        c.start()

    barrier = pltpu.get_barrier_semaphore()
    partners = quad[1:] + [far] + ring + xdev[1:] + [ydev]
    for dev in partners:
        pl.semaphore_signal(barrier, inc=1, device_id=dev, device_id_type=MESH)

    sent = []

    def remote(src, dst, sems, k, dev):
        return pltpu.make_async_remote_copy(
            src_ref=src, dst_ref=dst, send_sem=sems.at[0, k], recv_sem=sems.at[1, k],
            device_id=dev, device_id_type=MESH,
        )

    def start(c):
        c.start()
        sent.append(c)

    def c_w():
        return remote(wbuf.at[u, z], wbuf.at[u, z], w_sem, 0, far)

    def c_w_recv():
        return remote(wbuf.at[1 - u, z], wbuf.at[1 - u, z], w_sem, 0, far)

    def c_g(r):
        src, dst, dev = ((0, 1, quad[1]), (0, 2, quad[2]), (2, 3, quad[1]))[r - 1]
        return remote(gbuf.at[src], gbuf.at[dst], g_sem, r - 1, dev)

    def c_ag(d, h, j):
        uu = u if h == 0 else 1 - u
        zz = zoff(-DIRS[d] * j)
        return remote(wbuf.at[uu, zz], wbuf.at[uu, zz], ag_sem, MESSAGES.index((d, h, j)), ring[d])

    def c_ag_recv(d, h, j):
        uu = u if h == 0 else 1 - u
        zz = zoff(-DIRS[d] * (j + 1))
        return remote(wbuf.at[uu, zz], wbuf.at[uu, zz], ag_sem, MESSAGES.index((d, h, j)), ring[d])

    def c_x1():
        return remote(x_hbm.at[:, p, :, 1 - core], xbuf.at[1], x_sem, 0, quad[1])

    def c_x(r, o):
        pp, cc = quad_pc[r]
        zz = zoff(o)
        return remote(x_hbm.at[:, pp, zz, cc], xbuf.at[r, :, zz], x_sem, 1 + (r - 2) * NZ + o % NZ, quad[r])

    def c_o(r, o):
        zz = zoff(o)
        return remote(osend.at[r, o % NZ], ig_out.at[:, p, zz, core], o_sem, (r - 1) * NZ + o % NZ, quad[r])

    def c_o_recv(r, o):
        pp, cc = quad_pc[r]
        zz = zoff(o)
        return remote(osend.at[r, o % NZ], ig_out.at[:, pp, zz, cc], o_sem, (r - 1) * NZ + o % NZ, quad[r])

    def c_own(o):
        return pltpu.make_async_copy(osend.at[0, o % NZ], ig_out.at[:, p, zoff(o), core], own_sem.at[o % NZ])

    def c_rs(d, uu, r):
        k = SUMS.index((d, uu, r))
        return remote(rs_send.at[k], rs_recv.at[k], rs_sem, k, ring[d])

    def c_fin():
        return remote(fin_send.at[1 - u], fin_recv, fin_sem, 0, far)

    def c_ara(k):
        return remote(arw.at[xs[k]], ar_recv.at[k - 1], ar_sem, k - 1, xdev[k])

    def c_arb():
        return remote(ar_mid, ar_mid_recv, ar_sem, 3, ydev)

    def c_arc(k):
        return remote(ar_tot.at[ix], ar_tot.at[ix], ar_sem, 3 + k, xdev[k])

    def c_arc_recv(k):
        src = xs[NX - k]
        return remote(ar_tot.at[src], ar_tot.at[src], ar_sem, 3 + k, xdev[k])

    loads[0].wait()
    wbuf[u, z] = inner_v[frag[1]].astype(jnp.bfloat16)
    pl.semaphore_wait(barrier, len(partners))
    start(c_w())
    for d in range(2):
        start(c_ag(d, 0, 0))
    loads[1].wait()
    start(c_g(2))
    start(c_g(1))
    start(c_x1())
    for o in (4, 3, -3):
        for r in (2, 3):
            start(c_x(r, o))

    loads[3].wait()
    weighted = (outer_v[...] - inner_v[frag[0]]) / 8.0
    for k in range(NX):
        arw[k] = weighted[:, k * 128:(k + 1) * 128]
    for k in range(1, NX):
        start(c_ara(k))

    c_w_recv().wait_recv()
    for d in range(2):
        start(c_ag(d, 1, 0))

    c_g(2).wait_recv()
    start(c_g(3))
    c_g(1).wait_recv()
    c_g(3).wait_recv()
    g_all = gbuf[...].reshape(4 * TOK, KV)
    gt[...] = g_all.T
    loads[2].wait()
    c_x1().wait_recv()

    def partial(o):
        for r in (2, 3):
            c_x(r, o).wait_recv()
        zz = zoff(o)
        lhs = jnp.concatenate([xbuf[r, :, zz].reshape(2 * ROWS, TOK) for r in range(4)], axis=1)
        return jnp.dot(lhs, gbuf[...].reshape(4 * TOK, KV), preferred_element_type=jnp.float32)

    def send_sums(r):
        for d in range(2):
            o = DIRS[d] * (HALF - r)
            part = partial(o)
            for uu in sorted(range(2), key=lambda v: (d, v, r - 1) in SUMS):
                mine = part[uu * ROWS:(uu + 1) * ROWS]
                if (d, uu, r - 1) in SUMS:
                    c_rs(d, uu, r - 1).wait_recv()
                    mine = mine + rs_recv[SUMS.index((d, uu, r - 1))].astype(jnp.float32)
                rs_send[SUMS.index((d, uu, r))] = mine.astype(jnp.bfloat16)
                start(c_rs(d, uu, r))

    def forward(j):
        for h in range(2):
            for d in range(2):
                if (d, h, j - 1) in MESSAGES:
                    c_ag_recv(d, h, j - 1).wait_recv()
                if (d, h, j) in MESSAGES:
                    start(c_ag(d, h, j))

    def columns(o):
        zz = zoff(o)
        rows = wbuf[:, zz].reshape(2 * ROWS, KV)
        out = jnp.dot(rows, gt[...], preferred_element_type=jnp.float32).astype(jnp.bfloat16)
        for r in range(4):
            osend[r, o % NZ] = out[:, r * TOK:(r + 1) * TOK].reshape(2, ROWS, TOK)
        for r in (2, 3, 1):
            start(c_o(r, o))
        c_own(o).start()

    part = partial(4)
    for d in range(2):
        rs_send[SUMS.index((d, d, 0))] = part[d * ROWS:(d + 1) * ROWS].astype(jnp.bfloat16)
        start(c_rs(d, d, 0))
    for o in (2, -2):
        for r in (2, 3):
            start(c_x(r, o))
    forward(1)

    for k in range(1, NX):
        c_ara(k).wait_recv()
    ar_mid[...] = arw[ix] + ar_recv[0] + ar_recv[1] + ar_recv[2]
    start(c_arb())

    send_sums(1)
    for o in (1, -1, 0):
        for r in (2, 3):
            start(c_x(r, o))
    forward(2)
    columns(0)

    c_arb().wait_recv()
    ar_tot[ix] = ar_mid[...] + ar_mid_recv[...]
    for k in range(1, NX):
        start(c_arc(k))

    send_sums(2)
    forward(3)
    columns(1)
    columns(-1)
    send_sums(3)
    columns(2)
    columns(-2)

    part = partial(0)
    for uu in range(2):
        total = part[uu * ROWS:(uu + 1) * ROWS]
        for d in range(2):
            c_rs(d, uu, HALF - 1).wait_recv()
            total = total + rs_recv[SUMS.index((d, uu, HALF - 1))].astype(jnp.float32)
        fin[uu] = total
        fin_send[uu] = total.astype(jnp.bfloat16)
    start(c_fin())
    forward(4)
    columns(3)
    columns(-3)
    columns(4)

    for k in range(1, NX):
        c_arc_recv(k).wait_recv()
    loads[4].wait()
    for k in range(NX):
        cols = slice(k * 128, (k + 1) * 128)
        delta = ar_tot[k]
        new_momentum = 0.9 * mom_v[:, cols] + delta
        newmom_out[:, cols] = new_momentum
        par_out[:, cols] = outer_v[:, cols] - 0.7 * (delta + 0.9 * new_momentum)

    c_fin().wait_recv()
    wg_out[...] = fin[u] + fin_recv[...].astype(jnp.float32)
    for o in range(-3, 5):
        for r in (1, 2, 3):
            c_o_recv(r, o).wait_recv()
        c_own(o).wait()
    for c in sent:
        c.wait_send()


def local(act_t, cotangent, inner_params, outer_params, momentum, frag_index):
    bf16, f32 = jnp.bfloat16, jnp.float32
    any_space = pl.BlockSpec(memory_space=pl.ANY)
    vmem = pl.BlockSpec(memory_space=pltpu.VMEM)
    shape6 = (2, 2, NZ, 2, ROWS, TOK)
    dma = pltpu.SemaphoreType.DMA
    wg, ig, par, newmom = pl.pallas_call(
        kernel,
        out_shape=(
            jax.ShapeDtypeStruct((ROWS, KV), f32),
            jax.ShapeDtypeStruct(shape6, bf16),
            jax.ShapeDtypeStruct((ROWS, KV), f32),
            jax.ShapeDtypeStruct((ROWS, KV), f32),
        ),
        in_specs=[pl.BlockSpec(memory_space=pltpu.SMEM)] + [any_space] * 5,
        out_specs=(vmem, any_space, vmem, vmem),
        scratch_shapes=[
            pltpu.VMEM((4, ROWS, KV), f32),
            pltpu.VMEM((ROWS, KV), f32),
            pltpu.VMEM((ROWS, KV), f32),
            pltpu.VMEM((4, TOK, KV), bf16),
            pltpu.VMEM((KV, 4 * TOK), bf16),
            pltpu.VMEM((4, 2, NZ, ROWS, TOK), bf16),
            pltpu.VMEM((2, NZ, ROWS, KV), bf16),
            pltpu.VMEM((4, NZ, 2, ROWS, TOK), bf16),
            pltpu.VMEM((len(SUMS), ROWS, KV), bf16),
            pltpu.VMEM((len(SUMS), ROWS, KV), bf16),
            pltpu.VMEM((2, ROWS, KV), f32),
            pltpu.VMEM((2, ROWS, KV), bf16),
            pltpu.VMEM((ROWS, KV), bf16),
            pltpu.VMEM((NX, ROWS, 128), f32),
            pltpu.VMEM((NX - 1, ROWS, 128), f32),
            pltpu.VMEM((ROWS, 128), f32),
            pltpu.VMEM((ROWS, 128), f32),
            pltpu.VMEM((NX, ROWS, 128), f32),
            dma((5,)),
            dma((2, 1)),
            dma((2, 3)),
            dma((2, len(MESSAGES))),
            dma((2, 1 + 2 * NZ)),
            dma((2, 3 * NZ)),
            dma((2, len(SUMS))),
            dma((2, 1)),
            dma((2, 7)),
            dma((NZ,)),
        ],
        compiler_params=pltpu.CompilerParams(
            collective_id=0, has_side_effects=True, vmem_limit_bytes=40 * 2**20
        ),
        cost_estimate=pl.CostEstimate(flops=1700000000, bytes_accessed=6000000, transcendentals=0),
    )(
        frag_index,
        act_t.reshape(shape6),
        cotangent,
        inner_params,
        outer_params,
        momentum,
    )
    return wg[None], ig.reshape(act_t.shape), par, newmom


def solution(mesh):
    in_specs = (
        P(None, ("island", "fsdp")),
        P(("island", "fsdp"), None),
        P("island", None, "fsdp", None),
        P("fsdp", None),
        P("fsdp", None),
        P(),
    )
    out_specs = (
        P("island", "fsdp", None),
        P(None, ("island", "fsdp")),
        P("fsdp", None),
        P("fsdp", None),
    )
    return jax.shard_map(local, mesh=mesh, in_specs=in_specs, out_specs=out_specs, check_vma=False)
```

time: 305 us -> 74.9 us (0.25)
  waiting for transfers between devices: 251 us -> 0 us
  Pallas kernels: 0 us -> 64.9 us
  between operations: 19.4 us -> 0.66 us
  starting transfers between devices: 15.7 us -> 0 us
  matrix products: 11.2 us -> 0 us
  local copies, waits for them, and re-layouts: 2.92 us -> 9.12 us
  other arithmetic: 3.45 us -> 0 us
    all_gather x2 -> x0, waiting for transfers between devices: 150 us -> none  [the longest x1 119 us: local(): lax.all_gather(cotangent, 'fsdp', axis=0, tiled=True)]
    psum x1 -> x0, waiting for transfers between devices: 100 us -> none  [local(): delta = lax.psum(weighted, 'island')]
    pallas_call x0 -> x1, Pallas kernels: none -> 64.9 us  [local(): pl.pallas_call(kernel, out_shape=(jax.ShapeDtypeStruct((ROWS, KV), f32),...]
    all_to_all x1 -> x0, starting transfers between devices: 15.6 us -> none  [local(): lax.all_to_all(act_t, 'fsdp', split_axis=0, concat_axis=1, tiled=True)]
    dot_general x2 -> x0, matrix products: 11.2 us -> none  [the longest x1 5.72 us: local(): lax.dot_general(lax.all_gather(trained, 'fsdp', axis=0, tiled=True), cota...]
    unnamed x6 -> x16, local copies, waits for them, and re-layouts: 0.02 us -> 9.12 us
  transfers between devices with their start and end apart: 4 -> 0, of which waited for: 3 -> 0; matrix products, arithmetic and copies ran while one was open for 3% -> 0% of each run, Pallas kernels for 0% -> 0%
where the time goes in v1:
time: 74.9 us; the launch traced here: 74.7 us
  Pallas kernels  64.9 us (87%)
  local copies, waits for them, and re-layouts  9.12 us (12%)
    pallas_call x1, Pallas kernels, local(): pl.pallas_call(kernel, out_shape=(jax.ShapeDtypeStruct((ROWS, KV), f32),...  64.9 us
    unnamed x16, local copies, waits for them, and re-layouts  9.12 us

profile of v1, /device:TPU:1, one launch (start us, length us, event | category | flops | bytes accessed | tf_op | source)
XLA Modules:
  0.0 74.7 jit_solution(3712393841283550427)
XLA Ops:
  0.6 0.0 copy-start
  0.6 1.4 %copy-done = bf16[6144,128]{1,0:T(8,128)(2,1)S(1)} copy-done((bf16[6144,128]{1,0:T(8,128)(2,1)S(1)}, bf16[6144,128]{1,0:T(8,128)(2,1)}, u32[]{:S(2)}) %copy-start) | copy-done | bytes 1572888
  2.0 0.0 copy-start.1
  2.0 1.1 %copy-done.1 = f32[1,4,96,512]{3,2,1,0:T(8,128)S(1)} copy-done((f32[1,4,96,512]{3,2,1,0:T(8,128)S(1)}, f32[1,4,96,512]{3,2,1,0:T(8,128)}, u32[]{:S(2)}) %copy-start.1) | copy-done | bytes 786456
  3.2 0.0 copy-start.2
  3.2 0.9 %copy-done.2 = f32[96,512]{1,0:T(8,128)S(1)} copy-done((f32[96,512]{1,0:T(8,128)S(1)}, f32[96,512]{1,0:T(8,128)}, u32[]{:S(2)}) %copy-start.2) | copy-done | bytes 196632
  4.1 0.0 copy-start.3
  4.1 0.9 %copy-done.3 = f32[96,512]{1,0:T(8,128)S(1)} copy-done((f32[96,512]{1,0:T(8,128)S(1)}, f32[96,512]{1,0:T(8,128)}, u32[]{:S(2)}) %copy-start.3) | copy-done | bytes 196632
  5.0 0.0 copy-start.4
  5.0 0.9 %copy-done.4 = bf16[128,512]{1,0:T(8,128)(2,1)S(1)} copy-done((bf16[128,512]{1,0:T(8,128)(2,1)S(1)}, bf16[128,512]{1,0:T(8,128)(2,1)}, u32[]{:S(2)}) %copy-start.4) | copy-done | bytes 131096
  5.9 0.0 copy-start.5
  5.9 0.7 copy-done.5
  6.6 64.9 %shard_map.93 = (f32[96,512]{1,0:T(8,128)S(1)}, bf16[2,2,8,2,96,128]{5,4,3,2,1,0:T(8,128)(2,1)S(1)}, f32[96,512]{1,0:T(8,128)S(1)}, f32[96,512]{1,0:T(8,128)S(1)}) custom-call(s32[4]{0:T(128)S(1)} %copy-done.5, bf16[2,2,8,2,96,128]{5,4,3,2,1,0:T(8,128)(2,1)S(1)} %bitcast.5, bf16[128,512]{1,0:T(8,128)(2,1)S(1)} %copy-done.4, f32[1,4,96,512]{3,2,1,0:T(8,128)S(1)} %copy-done.1, ...), custom_call_target="tpu_custom_call" | custom-call | flops 1700000000 | bytes 6000000 | tf_op jit(solution)/shard_map/pallas_call | solution.py:290
  71.5 0.7 copy.14
  72.2 1.1 %copy.15 = bf16[6144,128]{1,0:T(8,128)(2,1)} copy(bf16[6144,128]{1,0:T(8,128)(2,1)S(1)} %bitcast.3) | data formatting | bytes 3145728
  73.3 0.7 copy.16
  74.0 0.7 copy.17
Async XLA Ops:
  0.6 1.4 %copy-start = (bf16[6144,128]{1,0:T(8,128)(2,1)S(1)}, bf16[6144,128]{1,0:T(8,128)(2,1)}, u32[]{:S(2)}) copy-start(bf16[6144,128]{1,0:T(8,128)(2,1)} %param.6) | copy-start | bytes 4718596
  2.0 1.1 %copy-start.1 = (f32[1,4,96,512]{3,2,1,0:T(8,128)S(1)}, f32[1,4,96,512]{3,2,1,0:T(8,128)}, u32[]{:S(2)}) copy-start(f32[1,4,96,512]{3,2,1,0:T(8,128)} %inner_hbm.1) | copy-start | bytes 2359300
  3.2 0.9 %copy-start.2 = (f32[96,512]{1,0:T(8,128)S(1)}, f32[96,512]{1,0:T(8,128)}, u32[]{:S(2)}) copy-start(f32[96,512]{1,0:T(8,128)} %outer_hbm.1) | copy-start | bytes 589828
  4.1 0.9 %copy-start.3 = (f32[96,512]{1,0:T(8,128)S(1)}, f32[96,512]{1,0:T(8,128)}, u32[]{:S(2)}) copy-start(f32[96,512]{1,0:T(8,128)} %mom_hbm.1) | copy-start | bytes 589828
  5.0 0.9 %copy-start.4 = (bf16[128,512]{1,0:T(8,128)(2,1)S(1)}, bf16[128,512]{1,0:T(8,128)(2,1)}, u32[]{:S(2)}) copy-start(bf16[128,512]{1,0:T(8,128)(2,1)} %g_hbm.1) | copy-start | bytes 393220
  5.9 0.7 copy-start.5

commit v2 on v1

v2 whole, which is shorter than its diff:
```python
import jax
import jax.numpy as jnp
from jax import lax
from jax.experimental import pallas as pl
from jax.experimental.pallas import tpu as pltpu
from jax.sharding import PartitionSpec as P

MESH = pl.DeviceIdType.MESH
KV = 512
TOK = 128
ROWS = 96
NZ = 8
NX = 4
HALF = NZ // 2
DIRS = (1, -1)


def chain(d, h):
    return HALF if d == h else HALF - 1


MESSAGES = [(d, h, j) for d in range(2) for h in range(2) for j in range(HALF) if j < chain(d, h)]
SUMS = [(d, h, r) for d in range(2) for h in range(2) for r in range(HALF) if HALF - r <= chain(d, h)]
PAIR = 64
REST = ROWS - PAIR

PLAN = (
    ("G", 1), ("G", 2), ("X1", 0), ("A0",), ("X1", 1), ("X", 1, 4), ("X", 1, 3), ("X", 1, -3), ("W",),
    ("X", 1, 2), ("X", 1, -2), ("R1",), ("GS",), ("s", 1, 1, 0), ("X0",), ("s", 0, 0, 0), ("s", 0, 1, 1),
    ("s", 1, 0, 1), ("G3",), ("GP",), ("S", 1, 1, 0), ("S", 0, 1, 1), ("X", 1, 1), ("X", 1, -1),
    ("X", 1, 0), ("X", 0, 4), ("F", 0, 0, 1), ("F", 1, 0, 1), ("s", 1, 1, 1), ("s", 0, 0, 1), ("FW",),
    ("S", 1, 1, 1), ("X", 0, 3), ("X", 0, -3), ("X", 0, 2), ("R2",), ("C", 0), ("F", 0, 0, 2),
    ("F", 1, 0, 2), ("s", 0, 1, 2), ("s", 1, 1, 2), ("s", 0, 0, 2), ("s", 1, 0, 2), ("S", 0, 1, 2),
    ("S", 1, 1, 2), ("X", 0, -2), ("X", 0, 1), ("X", 0, -1), ("X", 0, 0), ("F", 0, 1, 1), ("F", 1, 1, 1),
    ("C", -1), ("C", 1), ("R3",), ("S", 0, 0, 0), ("s", 0, 1, 3), ("s", 1, 1, 3), ("s", 0, 0, 3),
    ("s", 1, 0, 3), ("S", 0, 1, 3), ("S", 1, 1, 3), ("S", 1, 0, 1), ("S", 0, 0, 1), ("F", 0, 0, 3),
    ("F", 1, 0, 3), ("F", 0, 1, 2), ("F", 1, 1, 2), ("C", -2), ("C", 2), ("l", 1), ("l", 0), ("L", 1),
    ("S", 0, 0, 2), ("S", 1, 0, 2), ("F", 0, 1, 3), ("F", 1, 1, 3), ("F", 0, 0, 4), ("F", 1, 0, 4),
    ("C", -3), ("C", 3), ("S", 0, 0, 3), ("S", 1, 0, 3), ("F", 0, 1, 4), ("F", 1, 1, 4), ("C", 4), ("R4",),
    ("L", 0),
)


def kernel(
    frag, x_hbm, g_hbm, inner_hbm, outer_hbm, mom_hbm,
    wg_out, ig_out, par_out, newmom_out,
    inner_v, outer_v, mom_v, gbuf, gt, xbuf, xrest, wbuf, osend, rs_send, rs_recv, fin_send, fin_recv,
    ss_send, ss_recv, rest_tot, rest_send, rest_recv,
    arw, ar_recv, ar_mid, ar_mid_recv, ar_tot,
    local_sem, w_sem, g_sem, ag_sem, x_sem, o_sem, rs_sem, ss_sem, fin_sem, ar_sem,
):
    island = lax.axis_index("island")
    me = lax.axis_index("fsdp")
    core = lax.rem(me, 2)
    z = lax.rem(me // 2, NZ)
    y = me // (2 * NZ)
    u = y // 2
    p = lax.rem(y, 2)
    half = (u, 1 - u)
    ix = island // 2
    iy = lax.rem(island, 2)

    def at(yy, zz, cc):
        return (island, (yy * NZ + zz) * 2 + cc)

    def zoff(o):
        return lax.rem(z + (o + NZ), NZ)

    y_pair = y + 1 - 2 * p
    quad = [None, at(y, z, 1 - core), at(y_pair, z, core), at(y_pair, z, 1 - core)]
    quad_pc = [(p, core), (p, 1 - core), (1 - p, core), (1 - p, 1 - core)]
    far = at(lax.rem(y + 2, 4), z, core)
    cross = at(3 - y, z, core)
    ring = [at(y, zoff(1), core), at(y, zoff(-1), core)]
    xs = [lax.rem(ix + k, NX) for k in range(NX)]
    xdev = [None] + [(xs[k] * 2 + iy, me) for k in range(1, NX)]
    ydev = (ix * 2 + 1 - iy, me)

    loads = [
        pltpu.make_async_copy(inner_hbm.at[0], inner_v, local_sem.at[0]),
        pltpu.make_async_copy(g_hbm, gbuf.at[0], local_sem.at[1]),
        pltpu.make_async_copy(x_hbm.at[:, p, :, core], xbuf.at[0], local_sem.at[2]),
        pltpu.make_async_copy(outer_hbm, outer_v, local_sem.at[3]),
        pltpu.make_async_copy(mom_hbm, mom_v, local_sem.at[4]),
        pltpu.make_async_copy(x_hbm.at[:, 1 - p, :, core, PAIR:], xrest.at[0], local_sem.at[5]),
    ]
    for c in loads:
        c.start()

    barrier = pltpu.get_barrier_semaphore()
    partners = quad[1:] + [far, cross] + ring + xdev[1:] + [ydev]
    for dev in partners:
        pl.semaphore_signal(barrier, inc=1, device_id=dev, device_id_type=MESH)

    sent = []

    def remote(src, dst, sems, k, dev):
        return pltpu.make_async_remote_copy(
            src_ref=src, dst_ref=dst, send_sem=sems.at[0, k], recv_sem=sems.at[1, k],
            device_id=dev, device_id_type=MESH,
        )

    def start(c):
        c.start()
        sent.append(c)

    def c_w():
        return remote(wbuf.at[u, z], wbuf.at[u, z], w_sem, 0, far)

    def c_w_recv():
        return remote(wbuf.at[1 - u, z], wbuf.at[1 - u, z], w_sem, 0, far)

    def c_g(r):
        src, dst, dev = ((0, 1, quad[1]), (0, 2, quad[2]), (2, 3, quad[1]))[r - 1]
        return remote(gbuf.at[src], gbuf.at[dst], g_sem, r - 1, dev)

    def c_ag(d, h, j):
        zz = zoff(-DIRS[d] * j)
        return remote(wbuf.at[half[h], zz], wbuf.at[half[h], zz], ag_sem, MESSAGES.index((d, h, j)), ring[d])

    def c_ag_recv(d, h, j):
        zz = zoff(-DIRS[d] * (j + 1))
        return remote(wbuf.at[half[h], zz], wbuf.at[half[h], zz], ag_sem, MESSAGES.index((d, h, j)), ring[d])

    def c_x1(k):
        if k == 0:
            return remote(x_hbm.at[:, 1 - p, :, 1 - core, PAIR:], xrest.at[1], x_sem, 0, quad[1])
        return remote(x_hbm.at[:, p, :, 1 - core], xbuf.at[1], x_sem, 1, quad[1])

    def c_x(r, h, o):
        pp, cc = quad_pc[r]
        zz = zoff(o)
        k = 2 + ((r - 2) * 2 + h) * NZ + o % NZ
        rows = pl.ds(0, PAIR)
        return remote(x_hbm.at[half[h], pp, zz, cc, rows], xbuf.at[r, half[h], zz, rows], x_sem, k, quad[r])

    def c_o(r, o):
        zz = zoff(o)
        return remote(osend.at[r, o % NZ], ig_out.at[:, p, zz, core], o_sem, (r - 1) * NZ + o % NZ, quad[r])

    def c_o_recv(r, o):
        pp, cc = quad_pc[r]
        zz = zoff(o)
        return remote(osend.at[r, o % NZ], ig_out.at[:, pp, zz, cc], o_sem, (r - 1) * NZ + o % NZ, quad[r])

    def c_rs(d, h, r):
        k = SUMS.index((d, h, r))
        return remote(rs_send.at[k], rs_recv.at[k], rs_sem, k, ring[d])

    def c_ss(d, h, r):
        k = SUMS.index((d, h, r))
        return remote(ss_send.at[k], ss_recv.at[k], ss_sem, k, ring[d])

    def c_fin(k):
        if k == 0:
            return remote(fin_send, fin_recv, fin_sem, 0, far)
        src = rest_send.at[0, 1 - u] if k == 1 else rest_send.at[1, u if k == 2 else 1 - u]
        return remote(src, rest_recv.at[k - 1], fin_sem, k, (far, quad[2], cross)[k - 1])

    def c_ara(k):
        return remote(arw.at[xs[k]], ar_recv.at[k - 1], ar_sem, k - 1, xdev[k])

    def c_arb():
        return remote(ar_mid, ar_mid_recv, ar_sem, 3, ydev)

    def c_arc(k):
        return remote(ar_tot.at[ix], ar_tot.at[ix], ar_sem, 3 + k, xdev[k])

    def c_arc_recv(k):
        src = xs[NX - k]
        return remote(ar_tot.at[src], ar_tot.at[src], ar_sem, 3 + k, xdev[k])

    loads[0].wait()
    wbuf[u, z] = inner_v[frag[1]].astype(jnp.bfloat16)
    pl.semaphore_wait(barrier, len(partners))

    def product(lhs, members):
        g = gbuf[0:members].reshape(members * TOK, KV)
        return jnp.dot(lhs, g, preferred_element_type=jnp.float32)

    def pair_part(h, o):
        for r in (2, 3):
            c_x(r, h, o).wait_recv()
        return product(jnp.concatenate([xbuf[r, half[h], zoff(o), 0:PAIR] for r in range(4)], axis=1), 4)

    def rest_part(b, o):
        if b == 0:
            lhs = [xbuf[r, :, zoff(o), PAIR:ROWS] for r in range(2)]
        else:
            lhs = [xrest[r, :, zoff(o)] for r in range(2)]
        return product(jnp.concatenate([v.reshape(2 * REST, TOK) for v in lhs], axis=1), 2)

    def add_and_send(part, copy, send, recv, d, h, r):
        mine = part(h, DIRS[d] * (HALF - r))
        if (d, h, r - 1) in SUMS:
            copy(d, h, r - 1).wait_recv()
            mine = mine + recv[SUMS.index((d, h, r - 1))].astype(jnp.float32)
        send[SUMS.index((d, h, r))] = mine.astype(jnp.bfloat16)
        start(copy(d, h, r))

    def last_sum(part, copy, recv, h):
        total = part(h, 0)
        for d in range(2):
            copy(d, h, HALF - 1).wait_recv()
            total = total + recv[SUMS.index((d, h, HALF - 1))].astype(jnp.float32)
        return total

    def do(op, *i):
        if op == "A0":
            for d in range(2):
                start(c_ag(d, 0, 0))
        elif op == "W":
            start(c_w())
        elif op == "FW":
            c_w_recv().wait_recv()
            for d in range(2):
                start(c_ag(d, 1, 0))
        elif op == "G":
            start(c_g(i[0]))
        elif op == "X1":
            start(c_x1(i[0]))
        elif op == "GS":
            c_g(1).wait_recv()
            loads[5].wait()
            c_x1(0).wait_recv()
        elif op == "G3":
            c_g(2).wait_recv()
            start(c_g(3))
        elif op == "GP":
            c_g(3).wait_recv()
            gt[...] = gbuf[...].reshape(4 * TOK, KV).T
        elif op == "X0":
            loads[2].wait()
            c_x1(1).wait_recv()
        elif op == "X":
            for r in (2, 3):
                start(c_x(r, *i))
        elif op == "s":
            add_and_send(rest_part, c_ss, ss_send, ss_recv, *i)
        elif op == "S":
            add_and_send(pair_part, c_rs, rs_send, rs_recv, *i)
        elif op == "l":
            total = last_sum(rest_part, c_ss, ss_recv, i[0]).reshape(2, REST, KV)
            if i[0] == 0:
                rest_tot[...] = total
            rest_send[i[0]] = total.astype(jnp.bfloat16)
            for k in ((1,), (2, 3))[i[0]]:
                start(c_fin(k))
        elif op == "L":
            total = last_sum(pair_part, c_rs, rs_recv, i[0])
            if i[0] == 1:
                fin_send[...] = total.astype(jnp.bfloat16)
                start(c_fin(0))
            else:
                wg_out[0:PAIR] = total
        elif op == "F":
            d, h, j = i
            if (d, h, j - 1) in MESSAGES:
                c_ag_recv(d, h, j - 1).wait_recv()
            if (d, h, j) in MESSAGES:
                start(c_ag(d, h, j))
        elif op == "C":
            o = i[0]
            rows = wbuf[:, zoff(o)].reshape(2 * ROWS, KV)
            out = jnp.dot(rows, gt[...], preferred_element_type=jnp.float32).astype(jnp.bfloat16)
            for r in range(1, 4):
                osend[r, o % NZ] = out[:, r * TOK:(r + 1) * TOK].reshape(2, ROWS, TOK)
            for r in (2, 3, 1):
                start(c_o(r, o))
            ig_out[:, p, zoff(o), core] = out[:, :TOK].reshape(2, ROWS, TOK)
        elif op == "R1":
            loads[3].wait()
            weighted = (outer_v[...] - inner_v[frag[0]]) / 8.0
            for k in range(NX):
                arw[k] = weighted[:, k * 128:(k + 1) * 128]
            for k in range(1, NX):
                start(c_ara(k))
        elif op == "R2":
            for k in range(1, NX):
                c_ara(k).wait_recv()
            ar_mid[...] = arw[ix] + ar_recv[0] + ar_recv[1] + ar_recv[2]
            start(c_arb())
        elif op == "R3":
            c_arb().wait_recv()
            ar_tot[ix] = ar_mid[...] + ar_mid_recv[...]
            for k in range(1, NX):
                start(c_arc(k))
        elif op == "R4":
            for k in range(1, NX):
                c_arc_recv(k).wait_recv()
            loads[4].wait()
            for k in range(NX):
                cols = slice(k * 128, (k + 1) * 128)
                delta = ar_tot[k]
                new_momentum = 0.9 * mom_v[:, cols] + delta
                newmom_out[:, cols] = new_momentum
                par_out[:, cols] = outer_v[:, cols] - 0.7 * (delta + 0.9 * new_momentum)

    loads[1].wait()
    for step in PLAN:
        do(*step)

    for k in range(4):
        c_fin(k).wait_recv()
    wg_out[0:PAIR] += fin_recv[...].astype(jnp.float32)
    rest = rest_tot[u]
    for k in range(3):
        rest = rest + rest_recv[k].astype(jnp.float32)
    wg_out[PAIR:ROWS] = rest
    for o in range(-3, 5):
        for r in (1, 2, 3):
            c_o_recv(r, o).wait_recv()
    for c in sent:
        c.wait_send()


def local(act_t, cotangent, inner_params, outer_params, momentum, frag_index):
    bf16, f32 = jnp.bfloat16, jnp.float32
    hbm = pl.BlockSpec(memory_space=pltpu.HBM)
    vmem = pl.BlockSpec(memory_space=pltpu.VMEM)
    shape6 = (2, 2, NZ, 2, ROWS, TOK)
    dma = pltpu.SemaphoreType.DMA
    wg, ig, par, newmom = pl.pallas_call(
        kernel,
        out_shape=(
            pltpu.VMEM((ROWS, KV), f32),
            pltpu.VMEM(shape6, bf16),
            pltpu.VMEM((ROWS, KV), f32),
            pltpu.VMEM((ROWS, KV), f32),
        ),
        in_specs=[pl.BlockSpec(memory_space=pltpu.SMEM)] + [hbm] * 5,
        out_specs=(vmem, vmem, vmem, vmem),
        scratch_shapes=[
            pltpu.VMEM((4, ROWS, KV), f32),
            pltpu.VMEM((ROWS, KV), f32),
            pltpu.VMEM((ROWS, KV), f32),
            pltpu.VMEM((4, TOK, KV), bf16),
            pltpu.VMEM((KV, 4 * TOK), bf16),
            pltpu.VMEM((4, 2, NZ, ROWS, TOK), bf16),
            pltpu.VMEM((2, 2, NZ, REST, TOK), bf16),
            pltpu.VMEM((2, NZ, ROWS, KV), bf16),
            pltpu.VMEM((4, NZ, 2, ROWS, TOK), bf16),
            pltpu.VMEM((len(SUMS), PAIR, KV), bf16),
            pltpu.VMEM((len(SUMS), PAIR, KV), bf16),
            pltpu.VMEM((PAIR, KV), bf16),
            pltpu.VMEM((PAIR, KV), bf16),
            pltpu.VMEM((len(SUMS), 2 * REST, KV), bf16),
            pltpu.VMEM((len(SUMS), 2 * REST, KV), bf16),
            pltpu.VMEM((2, REST, KV), f32),
            pltpu.VMEM((2, 2, REST, KV), bf16),
            pltpu.VMEM((3, REST, KV), bf16),
            pltpu.VMEM((NX, ROWS, 128), f32),
            pltpu.VMEM((NX - 1, ROWS, 128), f32),
            pltpu.VMEM((ROWS, 128), f32),
            pltpu.VMEM((ROWS, 128), f32),
            pltpu.VMEM((NX, ROWS, 128), f32),
            dma((6,)),
            dma((2, 1)),
            dma((2, 3)),
            dma((2, len(MESSAGES))),
            dma((2, 2 + 4 * NZ)),
            dma((2, 3 * NZ)),
            dma((2, len(SUMS))),
            dma((2, len(SUMS))),
            dma((2, 4)),
            dma((2, 7)),
        ],
        compiler_params=pltpu.CompilerParams(
            collective_id=0, has_side_effects=True, vmem_limit_bytes=56 * 2**20
        ),
        cost_estimate=pl.CostEstimate(flops=1700000000, bytes_accessed=6000000, transcendentals=0),
    )(
        frag_index,
        act_t.reshape(shape6),
        cotangent,
        inner_params,
        outer_params,
        momentum,
    )
    return wg[None], ig.reshape(act_t.shape), par, newmom


def solution(mesh):
    in_specs = (
        P(None, ("island", "fsdp")),
        P(("island", "fsdp"), None),
        P("island", None, "fsdp", None),
        P("fsdp", None),
        P("fsdp", None),
        P(),
    )
    out_specs = (
        P("island", "fsdp", None),
        P(None, ("island", "fsdp")),
        P("fsdp", None),
        P("fsdp", None),
    )
    return jax.shard_map(local, mesh=mesh, in_specs=in_specs, out_specs=out_specs, check_vma=False)
```

time: 74.9 us -> 66.9 us (0.89)
  local copies, waits for them, and re-layouts: 9.12 us -> 3.17 us
  Pallas kernels: 64.9 us -> 62.9 us
    unnamed x16 -> x4, local copies, waits for them, and re-layouts: 9.12 us -> 3.17 us
    pallas_call x1, Pallas kernels: 64.9 us -> 62.9 us  [local(): pl.pallas_call(kernel, out_shape=(pltpu.VMEM((ROWS, KV), f32), pltpu.VMEM...]
where the time goes in v2:
time: 66.9 us; the launch traced here: 66.7 us
  Pallas kernels  62.9 us (94%)
  local copies, waits for them, and re-layouts  3.17 us (5%)
    pallas_call x1, Pallas kernels, local(): pl.pallas_call(kernel, out_shape=(pltpu.VMEM((ROWS, KV), f32), pltpu.VMEM...  62.9 us
    unnamed x4, local copies, waits for them, and re-layouts  3.17 us

profile of v2, /device:TPU:1, one launch (start us, length us, event | category | flops | bytes accessed | tf_op | source)
XLA Modules:
  0.0 66.7 jit_solution(18078849157000110943)
XLA Ops:
  0.6 62.9 %shard_map.93 = (f32[96,512]{1,0:T(8,128)S(1)}, bf16[2,2,8,2,96,128]{5,4,3,2,1,0:T(8,128)(2,1)S(1)}, f32[96,512]{1,0:T(8,128)S(1)}, f32[96,512]{1,0:T(8,128)S(1)}) custom-call(s32[4]{0:T(128)} %frag.1, bf16[2,2,8,2,96,128]{5,4,3,2,1,0:T(8,128)(2,1)} %bitcast.5, bf16[128,512]{1,0:T(8,128)(2,1)} %g_hbm.1, f32[1,4,96,512]{3,2,1,0:T(8,128)} %inner_hbm.1, ...), custom_call_target="tpu_custom_call" | custom-call | flops 1700000000 | bytes 6000000 | tf_op jit(solution)/shard_map/pallas_call | solution.py:323
  63.6 0.7 %copy.14 = f32[1,96,512]{2,1,0:T(8,128)} copy(f32[1,96,512]{2,1,0:T(8,128)S(1)} %bitcast.4) | data formatting | bytes 393216
  64.2 1.1 %copy.15 = bf16[6144,128]{1,0:T(8,128)(2,1)} copy(bf16[6144,128]{1,0:T(8,128)(2,1)S(1)} %bitcast.3) | data formatting | bytes 3145728
  65.4 0.7 %copy.16 = f32[96,512]{1,0:T(8,128)} copy(f32[96,512]{1,0:T(8,128)S(1)} %get-tuple-element.14) | data formatting | bytes 393216
  66.1 0.7 %copy.17 = f32[96,512]{1,0:T(8,128)} copy(f32[96,512]{1,0:T(8,128)S(1)} %get-tuple-element.15) | data formatting | bytes 393216

commit v3 on v2

--- a/solution.py
+++ b/solution.py
@@ -25,19 +25,18 @@
 REST = ROWS - PAIR
 
 PLAN = (
-    ("G", 1), ("G", 2), ("X1", 0), ("A0",), ("X1", 1), ("X", 1, 4), ("X", 1, 3), ("X", 1, -3), ("W",),
-    ("X", 1, 2), ("X", 1, -2), ("R1",), ("GS",), ("s", 1, 1, 0), ("X0",), ("s", 0, 0, 0), ("s", 0, 1, 1),
-    ("s", 1, 0, 1), ("G3",), ("GP",), ("S", 1, 1, 0), ("S", 0, 1, 1), ("X", 1, 1), ("X", 1, -1),
-    ("X", 1, 0), ("X", 0, 4), ("F", 0, 0, 1), ("F", 1, 0, 1), ("s", 1, 1, 1), ("s", 0, 0, 1), ("FW",),
-    ("S", 1, 1, 1), ("X", 0, 3), ("X", 0, -3), ("X", 0, 2), ("R2",), ("C", 0), ("F", 0, 0, 2),
-    ("F", 1, 0, 2), ("s", 0, 1, 2), ("s", 1, 1, 2), ("s", 0, 0, 2), ("s", 1, 0, 2), ("S", 0, 1, 2),
-    ("S", 1, 1, 2), ("X", 0, -2), ("X", 0, 1), ("X", 0, -1), ("X", 0, 0), ("F", 0, 1, 1), ("F", 1, 1, 1),
-    ("C", -1), ("C", 1), ("R3",), ("S", 0, 0, 0), ("s", 0, 1, 3), ("s", 1, 1, 3), ("s", 0, 0, 3),
-    ("s", 1, 0, 3), ("S", 0, 1, 3), ("S", 1, 1, 3), ("S", 1, 0, 1), ("S", 0, 0, 1), ("F", 0, 0, 3),
-    ("F", 1, 0, 3), ("F", 0, 1, 2), ("F", 1, 1, 2), ("C", -2), ("C", 2), ("l", 1), ("l", 0), ("L", 1),
-    ("S", 0, 0, 2), ("S", 1, 0, 2), ("F", 0, 1, 3), ("F", 1, 1, 3), ("F", 0, 0, 4), ("F", 1, 0, 4),
-    ("C", -3), ("C", 3), ("S", 0, 0, 3), ("S", 1, 0, 3), ("F", 0, 1, 4), ("F", 1, 1, 4), ("C", 4), ("R4",),
-    ("L", 0),
+    ("X", 1, 4), ("A0",), ("G", 1), ("X1", 0), ("X", 1, -3), ("G", 2), ("X", 0, 3), ("W",), ("R1",),
+    ("X", 0, -2), ("X1", 1), ("GS",), ("s", 0, 1, 1), ("s", 1, 1, 0), ("X0",), ("s", 0, 0, 0),
+    ("s", 1, 0, 1), ("F", 0, 0, 1), ("F", 1, 0, 1), ("X", 1, 1), ("X", 1, 0), ("s", 0, 1, 2),
+    ("s", 1, 1, 1), ("G3",), ("R2",), ("s", 0, 0, 1), ("GP",), ("S", 1, 1, 0), ("s", 1, 0, 2),
+    ("F", 0, 0, 2), ("F", 1, 0, 2), ("X", 0, 2), ("X", 1, 2), ("s", 0, 1, 3), ("s", 1, 1, 2), ("X", 0, -1),
+    ("X", 1, -1), ("FW",), ("s", 0, 0, 2), ("S", 1, 1, 1), ("X", 0, 0), ("C", 0), ("s", 1, 0, 3), ("R3",),
+    ("F", 0, 0, 3), ("X", 1, 3), ("X", 0, 1), ("F", 1, 0, 3), ("X", 0, 4), ("s", 1, 1, 3), ("X", 0, -3),
+    ("F", 0, 1, 1), ("C", -1), ("X", 1, -2), ("s", 0, 0, 3), ("R4",), ("S", 0, 1, 1), ("F", 1, 1, 1),
+    ("C", 1), ("S", 0, 0, 0), ("F", 0, 0, 4), ("S", 1, 0, 1), ("F", 0, 1, 2), ("C", -2), ("l", 1),
+    ("S", 1, 1, 2), ("l", 0), ("F", 1, 1, 2), ("C", 2), ("S", 0, 1, 2), ("S", 1, 0, 2), ("S", 0, 0, 1),
+    ("S", 1, 1, 3), ("F", 0, 1, 3), ("C", -3), ("F", 1, 1, 3), ("C", 3), ("S", 0, 1, 3), ("S", 1, 0, 3),
+    ("S", 0, 0, 2), ("L", 1), ("F", 1, 1, 4), ("C", 4), ("S", 0, 0, 3), ("L", 0),
 )
 
 

time: 66.9 us -> 61.8 us (0.924)
  Pallas kernels: 62.9 us -> 57.8 us
    pallas_call x1, Pallas kernels: 62.9 us -> 57.8 us  [local(): pl.pallas_call(kernel, out_shape=(pltpu.VMEM((ROWS, KV), f32), pltpu.VMEM...]
where the time goes in v3:
time: 61.8 us; the launch traced here: 61.7 us
  Pallas kernels  57.8 us (94%)
  local copies, waits for them, and re-layouts  3.17 us (5%)
  between operations  0.64 us (1%)
    pallas_call x1, Pallas kernels, local(): pl.pallas_call(kernel, out_shape=(pltpu.VMEM((ROWS, KV), f32), pltpu.VMEM...  57.8 us
    unnamed x4, local copies, waits for them, and re-layouts  3.17 us

profile of v3, /device:TPU:1, one launch (start us, length us, event | category | flops | bytes accessed | tf_op | source)
XLA Modules:
  0.0 61.7 jit_solution(2661363942452267828)
XLA Ops:
  0.6 57.8 %shard_map.93 = (f32[96,512]{1,0:T(8,128)S(1)}, bf16[2,2,8,2,96,128]{5,4,3,2,1,0:T(8,128)(2,1)S(1)}, f32[96,512]{1,0:T(8,128)S(1)}, f32[96,512]{1,0:T(8,128)S(1)}) custom-call(s32[4]{0:T(128)} %frag.1, bf16[2,2,8,2,96,128]{5,4,3,2,1,0:T(8,128)(2,1)} %bitcast.5, bf16[128,512]{1,0:T(8,128)(2,1)} %g_hbm.1, f32[1,4,96,512]{3,2,1,0:T(8,128)} %inner_hbm.1, ...), custom_call_target="tpu_custom_call" | custom-call | flops 1700000000 | bytes 6000000 | tf_op jit(solution)/shard_map/pallas_call | solution.py:322
  58.5 0.7 %copy.14 = f32[1,96,512]{2,1,0:T(8,128)} copy(f32[1,96,512]{2,1,0:T(8,128)S(1)} %bitcast.4) | data formatting | bytes 393216
  59.2 1.1 %copy.15 = bf16[6144,128]{1,0:T(8,128)(2,1)} copy(bf16[6144,128]{1,0:T(8,128)(2,1)S(1)} %bitcast.3) | data formatting | bytes 3145728
  60.3 0.7 %copy.16 = f32[96,512]{1,0:T(8,128)} copy(f32[96,512]{1,0:T(8,128)S(1)} %get-tuple-element.14) | data formatting | bytes 393216
  61.0 0.7 %copy.17 = f32[96,512]{1,0:T(8,128)} copy(f32[96,512]{1,0:T(8,128)S(1)} %get-tuple-element.15) | data formatting | bytes 393216

commit v4 on v3

--- a/solution.py
+++ b/solution.py
@@ -25,29 +25,30 @@
 REST = ROWS - PAIR
 
 PLAN = (
-    ("X", 1, 4), ("A0",), ("G", 1), ("X1", 0), ("X", 1, -3), ("G", 2), ("X", 0, 3), ("W",), ("R1",),
-    ("X", 0, -2), ("X1", 1), ("GS",), ("s", 0, 1, 1), ("s", 1, 1, 0), ("X0",), ("s", 0, 0, 0),
-    ("s", 1, 0, 1), ("F", 0, 0, 1), ("F", 1, 0, 1), ("X", 1, 1), ("X", 1, 0), ("s", 0, 1, 2),
-    ("s", 1, 1, 1), ("G3",), ("R2",), ("s", 0, 0, 1), ("GP",), ("S", 1, 1, 0), ("s", 1, 0, 2),
-    ("F", 0, 0, 2), ("F", 1, 0, 2), ("X", 0, 2), ("X", 1, 2), ("s", 0, 1, 3), ("s", 1, 1, 2), ("X", 0, -1),
-    ("X", 1, -1), ("FW",), ("s", 0, 0, 2), ("S", 1, 1, 1), ("X", 0, 0), ("C", 0), ("s", 1, 0, 3), ("R3",),
-    ("F", 0, 0, 3), ("X", 1, 3), ("X", 0, 1), ("F", 1, 0, 3), ("X", 0, 4), ("s", 1, 1, 3), ("X", 0, -3),
-    ("F", 0, 1, 1), ("C", -1), ("X", 1, -2), ("s", 0, 0, 3), ("R4",), ("S", 0, 1, 1), ("F", 1, 1, 1),
-    ("C", 1), ("S", 0, 0, 0), ("F", 0, 0, 4), ("S", 1, 0, 1), ("F", 0, 1, 2), ("C", -2), ("l", 1),
-    ("S", 1, 1, 2), ("l", 0), ("F", 1, 1, 2), ("C", 2), ("S", 0, 1, 2), ("S", 1, 0, 2), ("S", 0, 0, 1),
-    ("S", 1, 1, 3), ("F", 0, 1, 3), ("C", -3), ("F", 1, 1, 3), ("C", 3), ("S", 0, 1, 3), ("S", 1, 0, 3),
-    ("S", 0, 0, 2), ("L", 1), ("F", 1, 1, 4), ("C", 4), ("S", 0, 0, 3), ("L", 0),
+    ("W",), ("G", 1), ("A0",), ("X1", 0), ("X", 0, 3), ("G", 2), ("X1", 1), ("X", 1, 4), ("X", 0, -3),
+    ("GS",), ("s", 1, 1, 0), ("s", 0, 1, 1), ("X0",), ("s", 1, 0, 1), ("s", 0, 0, 0), ("F", 0, 0, 1),
+    ("F", 1, 0, 1), ("X", 1, 0), ("R1",), ("s", 1, 1, 1), ("X", 0, 4), ("FW",), ("X", 0, 1), ("s", 1, 0, 2),
+    ("X", 0, -2), ("G3",), ("s", 0, 0, 1), ("X", 1, -3), ("X", 1, 3), ("GP",), ("s", 0, 1, 2), ("X", 1, -1),
+    ("s", 1, 1, 2), ("F", 0, 1, 1), ("S", 1, 1, 0), ("C", 0), ("S", 0, 0, 0), ("X", 1, 2), ("s", 1, 0, 3),
+    ("X", 1, -2), ("X", 0, 2), ("s", 0, 0, 2), ("F", 1, 1, 1), ("F", 0, 0, 2), ("S", 0, 1, 1), ("C", 1),
+    ("F", 0, 1, 2), ("S", 1, 1, 1), ("C", -2), ("C", -1), ("X", 0, 0), ("F", 1, 0, 2), ("F", 1, 1, 2),
+    ("X", 1, 1), ("R2",), ("s", 0, 1, 3), ("S", 0, 1, 2), ("X", 0, -1), ("s", 1, 1, 3), ("S", 1, 1, 2),
+    ("s", 0, 0, 3), ("S", 1, 0, 1), ("F", 1, 0, 3), ("C", 2), ("S", 0, 0, 1), ("F", 1, 1, 3),
+    ("F", 0, 1, 3), ("C", 3), ("F", 0, 0, 3), ("C", -3), ("S", 0, 1, 3), ("S", 1, 1, 3), ("R3",),
+    ("S", 1, 0, 2), ("l", 0), ("S", 0, 0, 2), ("l", 1), ("F", 1, 1, 4), ("F", 0, 0, 4), ("L", 1), ("C", 4),
+    ("S", 0, 0, 3), ("S", 1, 0, 3), ("R4",), ("L", 0),
 )
 
 
 def kernel(
     frag, x_hbm, g_hbm, inner_hbm, outer_hbm, mom_hbm,
-    wg_out, ig_out, par_out, newmom_out,
+    f_out, ig_out,
     inner_v, outer_v, mom_v, gbuf, gt, xbuf, xrest, wbuf, osend, rs_send, rs_recv, fin_send, fin_recv,
     ss_send, ss_recv, rest_tot, rest_send, rest_recv,
     arw, ar_recv, ar_mid, ar_mid_recv, ar_tot,
     local_sem, w_sem, g_sem, ag_sem, x_sem, o_sem, rs_sem, ss_sem, fin_sem, ar_sem,
 ):
+    wg_out, par_out, newmom_out = (f_out.at[k] for k in range(3))
     island = lax.axis_index("island")
     me = lax.axis_index("fsdp")
     core = lax.rem(me, 2)
@@ -319,16 +320,14 @@
     vmem = pl.BlockSpec(memory_space=pltpu.VMEM)
     shape6 = (2, 2, NZ, 2, ROWS, TOK)
     dma = pltpu.SemaphoreType.DMA
-    wg, ig, par, newmom = pl.pallas_call(
+    results, ig = pl.pallas_call(
         kernel,
         out_shape=(
-            pltpu.VMEM((ROWS, KV), f32),
+            pltpu.VMEM((3, ROWS, KV), f32),
             pltpu.VMEM(shape6, bf16),
-            pltpu.VMEM((ROWS, KV), f32),
-            pltpu.VMEM((ROWS, KV), f32),
         ),
         in_specs=[pl.BlockSpec(memory_space=pltpu.SMEM)] + [hbm] * 5,
-        out_specs=(vmem, vmem, vmem, vmem),
+        out_specs=(vmem, vmem),
         scratch_shapes=[
             pltpu.VMEM((4, ROWS, KV), f32),
             pltpu.VMEM((ROWS, KV), f32),
@@ -376,6 +375,7 @@
         outer_params,
         momentum,
     )
+    wg, par, newmom = results[0], results[1], results[2]
     return wg[None], ig.reshape(act_t.shape), par, newmom
 
 

time: 61.8 us -> 60.5 us (0.979)
  local copies, waits for them, and re-layouts: 3.17 us -> 1.97 us
    unnamed x4 -> x1, local copies, waits for them, and re-layouts: 3.17 us -> 1.15 us
    squeeze x0 -> x1, local copies, waits for them, and re-layouts: none -> 0.82 us  [local(): wg, par, newmom = (results[0], results[1], results[2])]
where the time goes in v4:
time: 60.5 us; the launch traced here: 60.3 us
  Pallas kernels  57.7 us (95%)
  local copies, waits for them, and re-layouts  1.97 us (3%)
  between operations  0.64 us (1%)
    pallas_call x1, Pallas kernels, local(): pl.pallas_call(kernel, out_shape=(pltpu.VMEM((3, ROWS, KV), f32), pltpu.V...  57.7 us

profile of v4, /device:TPU:1, one launch (start us, length us, event | category | flops | bytes accessed | tf_op | source)
XLA Modules:
  0.0 60.3 jit_solution(3639010541195081468)
XLA Ops:
  0.6 57.7 %shard_map.93 = (f32[3,96,512]{2,1,0:T(8,128)S(1)}, bf16[2,2,8,2,96,128]{5,4,3,2,1,0:T(8,128)(2,1)S(1)}) custom-call(s32[4]{0:T(128)} %frag.1, bf16[2,2,8,2,96,128]{5,4,3,2,1,0:T(8,128)(2,1)} %bitcast.7, bf16[128,512]{1,0:T(8,128)(2,1)} %g_hbm.1, f32[1,4,96,512]{3,2,1,0:T(8,128)} %inner_hbm.1, f32[96,512]{1,0:T(8,128)} %outer_hbm.1, f32[96,512]{1,0:T(8,128)} %mom_hbm.1), custom_call_target="tpu_custom_call" | custom-call | flops 1700000000 | bytes 6000000 | tf_op jit(solution)/shard_map/pallas_call | solution.py:323
  58.4 1.1 %copy.11 = bf16[6144,128]{1,0:T(8,128)(2,1)} copy(bf16[6144,128]{1,0:T(8,128)(2,1)S(1)} %bitcast.6) | data formatting | bytes 3145728
  59.5 0.8 %slice_bitcast_fusion = (f32[96,512]{1,0:T(8,128)}, f32[96,512]{1,0:T(8,128)}, f32[1,96,512]{2,1,0:T(8,128)}) fusion(f32[3,96,512]{2,1,0:T(8,128)S(1)} %get-tuple-element.6), kind=kLoop, calls=%fused_computation | loop fusion | bytes 1179648 | tf_op jit(solution)/shard_map/squeeze | solution.py:378

commit v5 on v4

--- a/solution.py
+++ b/solution.py
@@ -25,18 +25,18 @@
 REST = ROWS - PAIR
 
 PLAN = (
-    ("W",), ("G", 1), ("A0",), ("X1", 0), ("X", 0, 3), ("G", 2), ("X1", 1), ("X", 1, 4), ("X", 0, -3),
-    ("GS",), ("s", 1, 1, 0), ("s", 0, 1, 1), ("X0",), ("s", 1, 0, 1), ("s", 0, 0, 0), ("F", 0, 0, 1),
-    ("F", 1, 0, 1), ("X", 1, 0), ("R1",), ("s", 1, 1, 1), ("X", 0, 4), ("FW",), ("X", 0, 1), ("s", 1, 0, 2),
-    ("X", 0, -2), ("G3",), ("s", 0, 0, 1), ("X", 1, -3), ("X", 1, 3), ("GP",), ("s", 0, 1, 2), ("X", 1, -1),
-    ("s", 1, 1, 2), ("F", 0, 1, 1), ("S", 1, 1, 0), ("C", 0), ("S", 0, 0, 0), ("X", 1, 2), ("s", 1, 0, 3),
-    ("X", 1, -2), ("X", 0, 2), ("s", 0, 0, 2), ("F", 1, 1, 1), ("F", 0, 0, 2), ("S", 0, 1, 1), ("C", 1),
-    ("F", 0, 1, 2), ("S", 1, 1, 1), ("C", -2), ("C", -1), ("X", 0, 0), ("F", 1, 0, 2), ("F", 1, 1, 2),
-    ("X", 1, 1), ("R2",), ("s", 0, 1, 3), ("S", 0, 1, 2), ("X", 0, -1), ("s", 1, 1, 3), ("S", 1, 1, 2),
-    ("s", 0, 0, 3), ("S", 1, 0, 1), ("F", 1, 0, 3), ("C", 2), ("S", 0, 0, 1), ("F", 1, 1, 3),
-    ("F", 0, 1, 3), ("C", 3), ("F", 0, 0, 3), ("C", -3), ("S", 0, 1, 3), ("S", 1, 1, 3), ("R3",),
-    ("S", 1, 0, 2), ("l", 0), ("S", 0, 0, 2), ("l", 1), ("F", 1, 1, 4), ("F", 0, 0, 4), ("L", 1), ("C", 4),
-    ("S", 0, 0, 3), ("S", 1, 0, 3), ("R4",), ("L", 0),
+    ("W",), ("G", 1), ("X1", 0), ("X", 0, -3), ("Z",), ("A0",), ("X1", 1), ("G", 2), ("X", 1, 4),
+    ("X", 1, -2), ("GS",), ("s", 1, 1, 0), ("s", 0, 1, 1), ("R1",), ("X0",), ("X", 0, -2), ("s", 0, 0, 0),
+    ("s", 1, 0, 1), ("F", 1, 0, 1), ("X", 1, -3), ("F", 0, 0, 1), ("X", 1, 3), ("X", 0, 3), ("FW",),
+    ("s", 1, 1, 1), ("X", 1, 2), ("s", 0, 0, 1), ("R2",), ("G3",), ("X", 1, 0), ("X", 0, 4), ("s", 0, 1, 2),
+    ("F", 1, 0, 2), ("X", 0, 1), ("F", 0, 0, 2), ("X", 0, 2), ("GP",), ("S", 1, 1, 0), ("X", 1, -1),
+    ("F", 1, 1, 1), ("X", 0, 0), ("S", 0, 1, 1), ("X", 1, 1), ("C", 1), ("s", 0, 0, 2), ("s", 0, 1, 3),
+    ("F", 0, 1, 1), ("S", 0, 0, 0), ("S", 1, 1, 1), ("s", 1, 1, 2), ("C", 0), ("X", 0, -1), ("F", 1, 1, 2),
+    ("R3",), ("C", -1), ("C", 2), ("S", 1, 1, 2), ("S", 0, 1, 2), ("F", 0, 0, 3), ("s", 1, 1, 3),
+    ("S", 1, 0, 1), ("s", 1, 0, 2), ("F", 0, 1, 2), ("F", 1, 1, 3), ("C", -2), ("F", 1, 0, 3),
+    ("S", 0, 0, 1), ("R4",), ("l", 1), ("S", 0, 1, 3), ("C", 3), ("S", 1, 1, 3), ("s", 0, 0, 3),
+    ("s", 1, 0, 3), ("F", 0, 1, 3), ("F", 0, 0, 4), ("C", -3), ("S", 1, 0, 2), ("S", 0, 0, 2),
+    ("F", 1, 1, 4), ("L", 1), ("l", 0), ("C", 4), ("S", 0, 0, 3), ("S", 1, 0, 3), ("L", 0),
 )
 
 
@@ -46,7 +46,7 @@
     inner_v, outer_v, mom_v, gbuf, gt, xbuf, xrest, wbuf, osend, rs_send, rs_recv, fin_send, fin_recv,
     ss_send, ss_recv, rest_tot, rest_send, rest_recv,
     arw, ar_recv, ar_mid, ar_mid_recv, ar_tot,
-    local_sem, w_sem, g_sem, ag_sem, x_sem, o_sem, rs_sem, ss_sem, fin_sem, ar_sem,
+    local_sem, w_sem, g_sem, ag_sem, x_sem, o_sem, rs_sem, ss_sem, fin_sem, ar_sem, ready,
 ):
     wg_out, par_out, newmom_out = (f_out.at[k] for k in range(3))
     island = lax.axis_index("island")
@@ -88,9 +88,27 @@
         c.start()
 
     barrier = pltpu.get_barrier_semaphore()
-    partners = quad[1:] + [far, cross] + ring + xdev[1:] + [ydev]
+    def signal(sem, dev):
+        pl.semaphore_signal(sem, inc=1, device_id=dev, device_id_type=MESH)
+
+    partners = quad[1:] + [far, cross] + xdev[1:]
     for dev in partners:
-        pl.semaphore_signal(barrier, inc=1, device_id=dev, device_id_type=MESH)
+        signal(barrier, dev)
+
+    @pl.when(z < NZ - 1)
+    def _():
+        signal(barrier, ring[0])
+
+    @pl.when(z == 0)
+    def _():
+        signal(barrier, ring[1])
+
+    @pl.when(iy == 0)
+    def _():
+        signal(barrier, ydev)
+
+    after_z = jnp.minimum(z, 1)
+    at_end = z // (NZ - 1)
 
     sent = []
 
@@ -172,7 +190,20 @@
 
     loads[0].wait()
     wbuf[u, z] = inner_v[frag[1]].astype(jnp.bfloat16)
-    pl.semaphore_wait(barrier, len(partners))
+    pl.semaphore_wait(barrier, len(partners) + after_z + at_end + iy)
+
+    @pl.when(z > 0)
+    def _():
+        signal(ready.at[0], ring[1])
+
+    @pl.when(z == NZ - 1)
+    def _():
+        signal(ready.at[1], ring[0])
+
+    @pl.when(iy == 1)
+    def _():
+        signal(ready.at[2], ydev)
+
 
     def product(lhs, members):
         g = gbuf[0:members].reshape(members * TOK, KV)
@@ -206,7 +237,15 @@
         return total
 
     def do(op, *i):
-        if op == "A0":
+        if op == "Z":
+            @pl.when(z < NZ - 1)
+            def _():
+                pl.semaphore_wait(ready.at[0], 1)
+
+            @pl.when(z == 0)
+            def _():
+                pl.semaphore_wait(ready.at[1], 1)
+        elif op == "A0":
             for d in range(2):
                 start(c_ag(d, 0, 0))
         elif op == "W":
@@ -279,6 +318,11 @@
             for k in range(1, NX):
                 c_ara(k).wait_recv()
             ar_mid[...] = arw[ix] + ar_recv[0] + ar_recv[1] + ar_recv[2]
+
+            @pl.when(iy == 0)
+            def _():
+                pl.semaphore_wait(ready.at[2], 1)
+
             start(c_arb())
         elif op == "R3":
             c_arb().wait_recv()
@@ -362,6 +406,7 @@
             dma((2, len(SUMS))),
             dma((2, 4)),
             dma((2, 7)),
+            pltpu.SemaphoreType.REGULAR((3,)),
         ],
         compiler_params=pltpu.CompilerParams(
             collective_id=0, has_side_effects=True, vmem_limit_bytes=56 * 2**20

time: 60.5 us -> 57.9 us (0.957)
  Pallas kernels: 57.7 us -> 55.1 us
    pallas_call x1, Pallas kernels: 57.7 us -> 55.1 us  [local(): pl.pallas_call(kernel, out_shape=(pltpu.VMEM((3, ROWS, KV), f32), pltpu.V...]
where the time goes in v5:
time: 57.9 us; the launch traced here: 57.7 us
  Pallas kernels  55.1 us (95%)
  local copies, waits for them, and re-layouts  1.97 us (3%)
  between operations  0.64 us (1%)
    pallas_call x1, Pallas kernels, local(): pl.pallas_call(kernel, out_shape=(pltpu.VMEM((3, ROWS, KV), f32), pltpu.V...  55.1 us

profile of v5, /device:TPU:1, one launch (start us, length us, event | category | flops | bytes accessed | tf_op | source)
XLA Modules:
  0.0 57.7 jit_solution(4253534608535829849)
XLA Ops:
  0.6 55.1 %shard_map.93 = (f32[3,96,512]{2,1,0:T(8,128)S(1)}, bf16[2,2,8,2,96,128]{5,4,3,2,1,0:T(8,128)(2,1)S(1)}) custom-call(s32[4]{0:T(128)} %frag.1, bf16[2,2,8,2,96,128]{5,4,3,2,1,0:T(8,128)(2,1)} %bitcast.7, bf16[128,512]{1,0:T(8,128)(2,1)} %g_hbm.1, f32[1,4,96,512]{3,2,1,0:T(8,128)} %inner_hbm.1, f32[96,512]{1,0:T(8,128)} %outer_hbm.1, f32[96,512]{1,0:T(8,128)} %mom_hbm.1), custom_call_target="tpu_custom_call" | custom-call | flops 1700000000 | bytes 6000000 | tf_op jit(solution)/shard_map/pallas_call | solution.py:367
  55.8 1.1 %copy.11 = bf16[6144,128]{1,0:T(8,128)(2,1)} copy(bf16[6144,128]{1,0:T(8,128)(2,1)S(1)} %bitcast.6) | data formatting | bytes 3145728
  56.9 0.8 %slice_bitcast_fusion = (f32[96,512]{1,0:T(8,128)}, f32[96,512]{1,0:T(8,128)}, f32[1,96,512]{2,1,0:T(8,128)}) fusion(f32[3,96,512]{2,1,0:T(8,128)S(1)} %get-tuple-element.6), kind=kLoop, calls=%fused_computation | loop fusion | bytes 1179648 | tf_op jit(solution)/shard_map/squeeze | solution.py:423

commit v6 on v5

--- a/solution.py
+++ b/solution.py
@@ -25,18 +25,18 @@
 REST = ROWS - PAIR
 
 PLAN = (
-    ("W",), ("G", 1), ("X1", 0), ("X", 0, -3), ("Z",), ("A0",), ("X1", 1), ("G", 2), ("X", 1, 4),
+    ("G", 1), ("X1", 0), ("X", 0, -3), ("W",), ("Z",), ("A0",), ("X1", 1), ("G", 2), ("X", 1, 4),
     ("X", 1, -2), ("GS",), ("s", 1, 1, 0), ("s", 0, 1, 1), ("R1",), ("X0",), ("X", 0, -2), ("s", 0, 0, 0),
     ("s", 1, 0, 1), ("F", 1, 0, 1), ("X", 1, -3), ("F", 0, 0, 1), ("X", 1, 3), ("X", 0, 3), ("FW",),
     ("s", 1, 1, 1), ("X", 1, 2), ("s", 0, 0, 1), ("R2",), ("G3",), ("X", 1, 0), ("X", 0, 4), ("s", 0, 1, 2),
     ("F", 1, 0, 2), ("X", 0, 1), ("F", 0, 0, 2), ("X", 0, 2), ("GP",), ("S", 1, 1, 0), ("X", 1, -1),
     ("F", 1, 1, 1), ("X", 0, 0), ("S", 0, 1, 1), ("X", 1, 1), ("C", 1), ("s", 0, 0, 2), ("s", 0, 1, 3),
     ("F", 0, 1, 1), ("S", 0, 0, 0), ("S", 1, 1, 1), ("s", 1, 1, 2), ("C", 0), ("X", 0, -1), ("F", 1, 1, 2),
-    ("R3",), ("C", -1), ("C", 2), ("S", 1, 1, 2), ("S", 0, 1, 2), ("F", 0, 0, 3), ("s", 1, 1, 3),
-    ("S", 1, 0, 1), ("s", 1, 0, 2), ("F", 0, 1, 2), ("F", 1, 1, 3), ("C", -2), ("F", 1, 0, 3),
-    ("S", 0, 0, 1), ("R4",), ("l", 1), ("S", 0, 1, 3), ("C", 3), ("S", 1, 1, 3), ("s", 0, 0, 3),
+    ("C", -1), ("C", 2), ("S", 1, 1, 2), ("S", 0, 1, 2), ("F", 0, 0, 3), ("s", 1, 1, 3),
+    ("S", 1, 0, 1), ("s", 1, 0, 2), ("F", 0, 1, 2), ("F", 1, 1, 3), ("C", -2), ("R3",), ("F", 1, 0, 3),
+    ("S", 0, 0, 1), ("l", 1), ("S", 0, 1, 3), ("C", 3), ("S", 1, 1, 3), ("s", 0, 0, 3),
     ("s", 1, 0, 3), ("F", 0, 1, 3), ("F", 0, 0, 4), ("C", -3), ("S", 1, 0, 2), ("S", 0, 0, 2),
-    ("F", 1, 1, 4), ("L", 1), ("l", 0), ("C", 4), ("S", 0, 0, 3), ("S", 1, 0, 3), ("L", 0),
+    ("F", 1, 1, 4), ("L", 1), ("l", 0), ("C", 4), ("R4",), ("S", 0, 0, 3), ("S", 1, 0, 3), ("L", 0),
 )
 
 
@@ -188,8 +188,6 @@
         src = xs[NX - k]
         return remote(ar_tot.at[src], ar_tot.at[src], ar_sem, 3 + k, xdev[k])
 
-    loads[0].wait()
-    wbuf[u, z] = inner_v[frag[1]].astype(jnp.bfloat16)
     pl.semaphore_wait(barrier, len(partners) + after_z + at_end + iy)
 
     @pl.when(z > 0)
@@ -236,7 +234,12 @@
             total = total + recv[SUMS.index((d, h, HALF - 1))].astype(jnp.float32)
         return total
 
+    first_use = [step[0] for step in PLAN if step[0] in ("W", "A0", "R1")][0]
+
     def do(op, *i):
+        if op == first_use:
+            loads[0].wait()
+            wbuf[u, z] = inner_v[frag[1]].astype(jnp.bfloat16)
         if op == "Z":
             @pl.when(z < NZ - 1)
             def _():

time: 57.9 us -> 57.9 us (level)
  no operation moved by 1% of the time
where the time goes in v6:
time: 57.9 us; the launch traced here: 57.7 us
  Pallas kernels  55.1 us (95%)
  local copies, waits for them, and re-layouts  1.97 us (3%)
  between operations  0.64 us (1%)
    pallas_call x1, Pallas kernels, local(): pl.pallas_call(kernel, out_shape=(pltpu.VMEM((3, ROWS, KV), f32), pltpu.V...  55.1 us

profile of v6, /device:TPU:1, one launch (start us, length us, event | category | flops | bytes accessed | tf_op | source)
XLA Modules:
  0.0 57.7 jit_solution(167583705379166880)
XLA Ops:
  0.6 55.1 %shard_map.93 = (f32[3,96,512]{2,1,0:T(8,128)S(1)}, bf16[2,2,8,2,96,128]{5,4,3,2,1,0:T(8,128)(2,1)S(1)}) custom-call(s32[4]{0:T(128)} %frag.1, bf16[2,2,8,2,96,128]{5,4,3,2,1,0:T(8,128)(2,1)} %bitcast.7, bf16[128,512]{1,0:T(8,128)(2,1)} %g_hbm.1, f32[1,4,96,512]{3,2,1,0:T(8,128)} %inner_hbm.1, f32[96,512]{1,0:T(8,128)} %outer_hbm.1, f32[96,512]{1,0:T(8,128)} %mom_hbm.1), custom_call_target="tpu_custom_call" | custom-call | flops 1700000000 | bytes 6000000 | tf_op jit(solution)/shard_map/pallas_call | solution.py:370
  55.8 1.1 %copy.11 = bf16[6144,128]{1,0:T(8,128)(2,1)} copy(bf16[6144,128]{1,0:T(8,128)(2,1)S(1)} %bitcast.6) | data formatting | bytes 3145728
  56.9 0.8 %slice_bitcast_fusion = (f32[96,512]{1,0:T(8,128)}, f32[96,512]{1,0:T(8,128)}, f32[1,96,512]{2,1,0:T(8,128)}) fusion(f32[3,96,512]{2,1,0:T(8,128)S(1)} %get-tuple-element.6), kind=kLoop, calls=%fused_computation | loop fusion | bytes 1179648 | tf_op jit(solution)/shard_map/squeeze | solution.py:426
